TPU v7x, 32 devices: a whole 2x2x4 slice. The times are simulated.
32 devices in a mesh: groups: 2 (over y), adapter: 4 (over x, core), tensor: 4 (over z).
Axes of the slice: x: 2, y: 2, z: 4, core: 2. Of those that a mesh axis runs over, the one named last changes fastest.
Arguments:
- queries: bfloat16 [512, 8192], P(('groups', 'adapter'), 'tensor'), parts along dimension 0, may hold values from -6 to 6
- key_cache_rows: bfloat16 [512, 128, 1024], P(('groups', 'adapter'), None, 'tensor'), parts along dimension 0, may hold values from -6 to 6
- value_cache_rows: bfloat16 [512, 128, 1024], P(('groups', 'adapter'), None, 'tensor'), parts along dimension 0, may hold values from -6 to 6
- current_token_key: bfloat16 [512, 1024], P(('groups', 'adapter'), 'tensor'), parts along dimension 0, may hold values from -6 to 6
- current_token_value: bfloat16 [512, 1024], P(('groups', 'adapter'), 'tensor'), parts along dimension 0, may hold values from -6 to 6
- cache_valid_length: int32 [512], P(('groups', 'adapter')), parts along dimension 0, may hold values from 16 to 128, as said below
- request_adapter_index: int32 [512], P(('groups', 'adapter')), parts along dimension 0, may hold values from 0 to 31, as said below
- adapter_storage_slot: int32 [64], P('groups'), parts along dimension 0, may hold values from 0 to 31, as said below
- output_projection: bfloat16 [8192, 4096], P('tensor'), may hold values from -0.1875 to 0.1875
- adapter_down_weight: bfloat16 [32, 64, 8192], P('adapter', None, 'tensor'), may hold values from -0.25 to 0.25
- adapter_up_weight: bfloat16 [32, 64, 4096], P('adapter', None, 'tensor'), may hold values from -0.75 to 0.75
Outputs:
- layer_out: bfloat16 [512, 4096], P(('groups', 'adapter'), 'tensor'), parts along dimension 0
There are 2 independent parts, one for each index of `groups`. A program takes and returns all parts, laid end to end along the dimension named above; an argument that names none is the same for every part. Nothing has to cross between parts.
Inputs may be any that keep to these rules, and one draw needn't show every extreme that they name: `request_adapter_index`: of the requests of one adapter index, at most 32 use adapters whose slots lie at any one adapter index (slot // 8); some adapter index serves exactly 32 from every adapter index. `adapter_storage_slot`: A permutation: every slot holds one adapter. `cache_valid_length`: the first request of every adapter index has all 128 positions valid.
All inputs are finite; a program needn't handle non-finite values.
Results may differ from a plain program's by a relative error of at most 0.008.
Values may be sent and summed in bfloat16 or wider, within the bound.
A program may use at most 128 MiB of HBM per device.

v0:
```python
import jax
import jax.numpy as jnp
from jax import lax
from jax.sharding import PartitionSpec as P

QUERY_HEADS = 64
KV_HEADS = 8
HEAD_WIDTH = 128


def attend(
    queries,
    key_cache_rows,
    value_cache_rows,
    current_token_key,
    current_token_value,
    cache_valid_length,
):
    requests = queries.shape[0]
    per_group = QUERY_HEADS // KV_HEADS
    kv_local = current_token_key.shape[1] // HEAD_WIDTH
    span = key_cache_rows.shape[1]
    scaling = HEAD_WIDTH ** (-0.5)
    query_all = queries.reshape(requests, kv_local, per_group, HEAD_WIDTH)
    keys_all = key_cache_rows.reshape(requests, span, kv_local, HEAD_WIDTH)
    values_all = value_cache_rows.reshape(requests, span, kv_local, HEAD_WIDTH)
    fresh_key = current_token_key.reshape(requests, kv_local, HEAD_WIDTH)
    scores = (
        jnp.einsum("rkgd,rpkd->rkgp", query_all, keys_all, preferred_element_type=jnp.float32)
        * scaling
    )
    fresh = (
        jnp.einsum("rkgd,rkd->rkg", query_all, fresh_key, preferred_element_type=jnp.float32)
        * scaling
    )
    positions = jnp.arange(span, dtype=jnp.int32)
    usable = positions[None, :] < cache_valid_length[:, None]
    scores = jnp.where(usable[:, None, None, :], scores, -jnp.inf)
    largest = jnp.maximum(jnp.max(scores, axis=-1), fresh)
    weights = jnp.exp(scores - largest[..., None])
    self_weight = jnp.exp(fresh - largest)
    totals = jnp.sum(weights, axis=-1) + self_weight
    chances = (weights / totals[..., None]).astype(jnp.bfloat16)
    self_chance = (self_weight / totals).astype(jnp.bfloat16)
    blended = jnp.einsum("rkgp,rpkd->rkgd", chances, values_all, preferred_element_type=jnp.float32)
    fresh_value = current_token_value.reshape(requests, kv_local, 1, HEAD_WIDTH).astype(jnp.float32)
    blended = blended + self_chance.astype(jnp.float32)[..., None] * fresh_value
    return blended.reshape(requests, kv_local * per_group * HEAD_WIDTH).astype(jnp.bfloat16)


def find_slot(wanted, adapter_storage_slot):
    catalog = jnp.arange(adapter_storage_slot.shape[0], dtype=jnp.int32)
    return jnp.sum(
        jnp.where(wanted[:, None] == catalog[None, :], adapter_storage_slot[None, :], 0), axis=1
    )


def reduce_terms(layer_inputs, gathered_weight, adapter_down_weight):
    incomplete_value = jnp.einsum(
        "bz,wez->wbe", layer_inputs, adapter_down_weight, preferred_element_type=jnp.float32
    )
    return jnp.sum(jnp.where(gathered_weight[:, :, None], incomplete_value, 0.0), axis=0)


def raise_terms(reduced_rank_state, gathered_weight, adapter_up_weight):
    broadcast_rows = jnp.where(
        gathered_weight[:, :, None], reduced_rank_state[None, :, :], jnp.zeros((), jnp.bfloat16)
    )
    return jnp.einsum(
        "wtg,wgk->tk", broadcast_rows, adapter_up_weight, preferred_element_type=jnp.float32
    ).astype(jnp.bfloat16)


def body(
    queries,
    key_cache_rows,
    value_cache_rows,
    current_token_key,
    current_token_value,
    cache_valid_length,
    request_adapter_index,
    adapter_storage_slot,
    output_projection,
    adapter_down_weight,
    adapter_up_weight,
):
    attended = attend(
        queries,
        key_cache_rows,
        value_cache_rows,
        current_token_key,
        current_token_value,
        cache_valid_length,
    )
    requests = attended.shape[0]
    resident_count = adapter_down_weight.shape[0]
    catalog = jnp.arange(resident_count, dtype=jnp.int32)
    projected = jnp.dot(attended, output_projection, preferred_element_type=jnp.float32)
    share = lax.psum_scatter(projected, "tensor", scatter_dimension=1, tiled=True)
    every_rows, every_ids = (
        lax.all_gather(attended, "adapter", axis=0, tiled=True),
        lax.all_gather(request_adapter_index, "adapter", axis=0, tiled=True),
    )
    storage = find_slot(every_ids, adapter_storage_slot)
    holder = storage // resident_count
    local_index = storage % resident_count
    mine = holder == lax.axis_index("adapter")
    mine_count = mine.astype(jnp.int32)
    position = jnp.cumsum(mine_count) - mine_count
    slot_total = 2 * requests
    packing = (jnp.arange(slot_total, dtype=jnp.int32)[:, None] == position[None, :]) & mine[
        None, :
    ]
    compact_rows = jnp.dot(
        packing.astype(jnp.bfloat16), every_rows, preferred_element_type=jnp.float32
    ).astype(jnp.bfloat16)
    packed_ids = jnp.sum(jnp.where(packing, local_index[None, :] + 1, 0), axis=1) - 1
    gathered_weight = packed_ids[None, :] == catalog[:, None]
    reduced_portion = reduce_terms(compact_rows, gathered_weight, adapter_down_weight)
    reduced_rank_state = lax.psum(reduced_portion, "tensor").astype(jnp.bfloat16)
    raised_output = raise_terms(reduced_rank_state, gathered_weight, adapter_up_weight)
    unpacked = jnp.dot(
        packing.T.astype(jnp.bfloat16), raised_output, preferred_element_type=jnp.float32
    )
    adapted = lax.psum_scatter(
        unpacked.astype(jnp.bfloat16), "adapter", scatter_dimension=0, tiled=True
    ).astype(jnp.float32)
    return (share + adapted).astype(jnp.bfloat16)


def solution(mesh):
    in_specs = (
        P(("groups", "adapter"), "tensor"),
        P(("groups", "adapter"), None, "tensor"),
        P(("groups", "adapter"), None, "tensor"),
        P(("groups", "adapter"), "tensor"),
        P(("groups", "adapter"), "tensor"),
        P(("groups", "adapter")),
        P(("groups", "adapter")),
        P("groups"),
        P("tensor", None),
        P("adapter", None, "tensor"),
        P("adapter", None, "tensor"),
    )
    out_specs = P(("groups", "adapter"), "tensor")
    return jax.shard_map(body, mesh=mesh, in_specs=in_specs, out_specs=out_specs, check_vma=False)
```

profile of v0, /device:TPU:0, one launch (start us, length us, event | category | flops | bytes accessed | tf_op | source)
XLA Modules:
  0.0 93.6 jit_solution(3765007769041102589)
XLA Ops:
  7.4 0.0 copy-start
  7.4 0.0 all-gather.2.cloned.1.call-start
  7.4 0.9 iota_compare_fusion.2
  8.3 0.8 reshape.152
  9.0 0.8 reshape.141
  9.8 1.0 %copy.34 = bf16[8,8,16,128]{3,2,1,0:T(8,128)(2,1)S(1)} copy(bf16[8,8,16,128]{3,1,2,0:T(8,128)(2,1)} %bitcast.90) | data formatting | bytes 524288
  10.8 0.3 fusion.53
  11.1 0.1 copy.31
  11.2 4.6 %fusion.52 = (f32[64,2,8]{2,1,0:T(2,128)S(1)}, f32[64,2,8,128]{3,2,1,0:T(8,128)S(1)}) fusion(bf16[64,2,8,128]{3,2,1,0:T(8,128)(2,1)S(1)} %bitcast.88, pred[64,128]{1,0:T(8,128)(4,1)S(1)} %iota_compare_fusion.2, bf16[64,128,256]{2,1,0:T(8,128)(2,1)} %param.12), kind=kOutput, calls=%fused_computation.66 | convolution fusion | flops 33946624 | bytes 4993024 | tf_op jit(solution)/shard_map/rkgd,rpkd->rkgp/dot_general | solution.py:29
  15.8 0.1 copy.24
  15.9 0.1 copy.25
  16.0 0.4 fusion.22
  16.4 0.1 copy.26
  16.5 0.1 copy.27
  16.6 0.1 copy.29
  16.7 3.5 %fusion.17 = bf16[64,2,8,128]{3,2,1,0:T(8,128)(2,1)S(1)} fusion(f32[64,2,8,128]{3,2,1,0:T(8,128)S(1)} %get-tuple-element.11, f32[64,2,128]{2,1,0:T(2,128)S(1)} %reshape.141, f32[64,2,8]{2,1,0:T(2,128)S(1)} %copy.29, f32[64,2,8]{2,1,0:T(2,128)S(1)} %copy.27, f32[64,2,8]{2,1,0:T(2,128)S(1)} %copy.25, bf16[64,128,256]{2,1,0:T(8,128)(2,1)} %param.13), kind=kOutput, calls=%fused_computation.14 | convolution fusion | flops 34340864 | bytes 5058560 | tf_op jit(solution)/shard_map/rkgp,rpkd->rkgd/dot_general | solution.py:45
  20.2 0.8 copy.56
  21.0 0.0 all-gather.2.cloned.1.call-update
  21.0 0.0 copy-start.4
  21.0 0.0 copy-start.3
  21.0 0.0 copy-start.2
  21.0 0.0 reduce-scatter.3.cloned.1.call-start
  21.1 9.8 %fusion.50 = f32[64,4096]{1,0:T(8,128)} fusion(bf16[2048,4096]{1,0:T(8,128)(2,1)} %param.19, bf16[8,8,16,128]{3,2,1,0:T(8,128)(2,1)S(1)} %bitcast.86), kind=kOutput, calls=%fused_computation.65 | convolution fusion | flops 1073741824 | bytes 18087936 | tf_op jit(solution)/shard_map/dot_general | solution.py:98
  30.9 0.0 copy-start.1
  30.9 0.0 reduce-scatter.3.cloned.1.call-update
  30.9 0.0 reduce-scatter.5.cloned.1.call-start
  31.0 0.0 copy-done.4
  31.0 0.6 dynamic-slice
  32.2 0.0 copy-done.3
  32.2 0.2 dynamic-update-slice
  32.5 6.4 %all-reduce = s32[256]{0:T(256)S(1)} all-reduce(s32[256]{0:T(256)S(1)} %dynamic-update-slice), channel_id=1, replica_groups=mesh['groups'=2,'adapter'=4,'tensor'=4] {'adapter'}, use_global_device_ids=true, to_apply=%add | all-reduce | flops 256 | bytes 2048
  38.9 0.0 copy-done.2
  38.9 0.1 select_reduce_fusion.1
  39.0 0.3 reduce-window.9
  39.3 0.1 slice.7
  39.4 0.1 slice_reduce_fusion
  39.5 0.1 bitcast_subtract_fusion
  39.6 0.1 select_reduce_fusion
  39.7 1.0 %all-gather.2.cloned.1.call-done = bf16[256,2048]{1,0:T(8,128)(2,1)} async-done(((bf16[64,2048]{1,0:T(8,128)(2,1)}), bf16[256,2048]{1,0:T(8,128)(2,1)}) %all-gather.2.cloned.1.call-update) | async-done | bytes 1048592 | tf_op jit(solution)/shard_map/all_gather | solution.py:101
  40.7 0.0 copy-done
  40.7 2.2 %fusion.21 = f32[128,64]{0,1:T(8,128)S(1)} fusion(bf16[8,64,2048]{2,1,0:T(8,128)(2,1)S(1)} %copy-done, bf16[256,2048]{1,0:T(8,128)(2,1)} %all-gather.2.cloned.1.call-done, pred[8,128]{1,0:T(8,128)(4,1)S(1)} %iota_compare_fusion.3, s32[256]{0:T(256)S(1)} %get-tuple-element.5, pred[256]{0:T(512)(128)(4,1)S(1)} %get-tuple-element.6), kind=kOutput, calls=%fused_computation.17 | convolution fusion | flops 403103744 | bytes 3180800 | tf_op jit(solution)/shard_map/bz,wez->wbe/dot_general | solution.py:59
  42.9 20.0 %psum.7 = bf16[128,64]{0,1:T(8,128)(2,1)S(1)} all-reduce(f32[128,64]{0,1:T(8,128)S(1)} %fusion.21), channel_id=1, replica_groups=mesh['groups'=2,'adapter'=4,'tensor'=4] {'tensor'}, use_global_device_ids=true, to_apply=%region_8.9 | all-reduce | flops 8192 | bytes 49152 | tf_op jit(solution)/shard_map/psum | solution.py:120
  62.9 0.0 copy-done.1
  62.9 1.4 %convolution_convert_fusion.1 = bf16[256,1024]{1,0:T(8,128)(2,1)} fusion(bf16[8,64,1024]{2,1,0:T(8,128)(2,1)S(1)} %copy-done.1, pred[8,128]{1,0:T(8,128)(4,1)S(1)} %iota_compare_fusion.3, bf16[128,64]{0,1:T(8,128)(2,1)S(1)} %psum.7, s32[256]{0:T(256)S(1)} %get-tuple-element.5, pred[256]{0:T(512)(128)(4,1)S(1)} %get-tuple-element.6), kind=kOutput, calls=%fused_computation.8 | convolution fusion | flops 201850880 | bytes 1591552 | tf_op jit(solution)/shard_map/dot_general | solution.py:122
  64.3 0.0 reduce-scatter.5.cloned.1.call-update
  64.3 0.0 reduce-scatter.3.cloned.1.call-done
  64.3 20.2 %reduce-scatter.5.cloned.1.call-done = bf16[64,1024]{1,0:T(8,128)(2,1)} async-done(((bf16[256,1024]{1,0:T(8,128)(2,1)}), bf16[64,1024]{1,0:T(8,128)(2,1)}) %reduce-scatter.5.cloned.1.call-update) | async-done | bytes 131088 | tf_op jit(solution)/shard_map/reduce_scatter | solution.py:125
  84.5 1.7 %add_convert_fusion = bf16[64,1024]{1,0:T(8,128)(2,1)} fusion(f32[64,1024]{1,0:T(8,128)} %reduce-scatter.3.cloned.1.call-done, bf16[64,1024]{1,0:T(8,128)(2,1)} %reduce-scatter.5.cloned.1.call-done), kind=kLoop, calls=%fused_computation.22 | loop fusion | flops 196608 | bytes 524288 | tf_op jit(solution)/shard_map/convert_element_type | solution.py:128
  (7 shorter events, 0.1 us)
Async XLA Ops:
  7.4 33.3 %copy-start = (bf16[8,64,2048]{2,1,0:T(8,128)(2,1)S(1)}, bf16[8,64,2048]{2,1,0:T(8,128)(2,1)}, u32[]{:S(2)}) copy-start(bf16[8,64,2048]{2,1,0:T(8,128)(2,1)} %param.20) | copy-start | bytes 6291460
  7.4 33.3 %all-gather.2.cloned.1.call-start = ((), (), s32[]{:S(2)}) async-start(), calls=%async_computation.3 | async-start | bytes 1310720 | tf_op jit(solution)/shard_map/all_gather | solution.py:101
  21.0 10.0 %copy-start.4 = (u32[32]{0:T(128)S(1)}, u32[32]{0:T(128)}, u32[]{:S(2)}) copy-start(u32[32]{0:T(128)} %constant.51) | copy-start | bytes 388
  21.0 11.2 %copy-start.3 = (s32[64]{0:T(128)S(1)}, s32[64]{0:T(128)}, u32[]{:S(2)}) copy-start(s32[64]{0:T(128)} %param.17) | copy-start | bytes 772
  21.0 17.9 %copy-start.2 = (s32[32]{0:T(128)S(1)}, s32[32]{0:T(128)}, u32[]{:S(2)}) copy-start(s32[32]{0:T(128)} %param.18) | copy-start | bytes 388
  21.0 43.3 %reduce-scatter.3.cloned.1.call-start = ((), (), s32[]{:S(2)}) async-start(), calls=%async_computation.2 | async-start | bytes 1310720 | tf_op jit(solution)/shard_map/reduce_scatter | solution.py:99
  30.9 32.0 %copy-start.1 = (bf16[8,64,1024]{2,1,0:T(8,128)(2,1)S(1)}, bf16[8,64,1024]{2,1,0:T(8,128)(2,1)}, u32[]{:S(2)}) copy-start(bf16[8,64,1024]{2,1,0:T(8,128)(2,1)} %param.21) | copy-start | bytes 3145732
  30.9 53.6 %reduce-scatter.5.cloned.1.call-start = ((), (), s32[]{:S(2)}) async-start(), calls=%async_computation.4 | async-start | bytes 655360 | tf_op jit(solution)/shard_map/reduce_scatter | solution.py:125
Sparse Core Ops, SparseCore 0:
  21.1 19.5 all-gather.1
Sparse Core Ops, SparseCore 1:
  31.0 30.8 reduce-scatter.2
  64.4 20.1 reduce-scatter.4
where the time goes:
time: 94.1 us; the launch traced here: 93.6 us
  blocking collectives  26.4 us (28%)
  matrix products  21.7 us (23%)
  waiting for transfers between devices  21.2 us (23%)
  between operations  15.7 us (17%)
  local copies, waits for them, and re-layouts  4.92 us (5%)
  other arithmetic  3.65 us (4%)
    reduce_scatter x1, waiting for transfers between devices, body(): lax.psum_scatter(unpacked.astype(jnp.bfloat16), 'adapter', scatter_dimens...  20.2 us
    psum x1, blocking collectives, body(): lax.psum(reduced_portion, 'tensor').astype(jnp.bfloat16)  20 us
    dot_general x1, matrix products, body(): jnp.dot(attended, output_projection, preferred_element_type=jnp.float32)  9.78 us
    unnamed x1, blocking collectives  6.41 us
    dot_general x1, matrix products, attend(): jnp.einsum('rkgd,rpkd->rkgp', query_all, keys_all, preferred_element_type...  4.59 us
    dot_general x1, matrix products, attend(): jnp.einsum('rkgp,rpkd->rkgd', chances, values_all, preferred_element_type...  3.46 us
    unnamed x15, local copies, waits for them, and re-layouts  2.62 us
    dot_general x1, matrix products, reduce_terms(): jnp.einsum('bz,wez->wbe', layer_inputs, adapter_down_weight, preferred_el...  2.16 us
  transfers between devices with their start and end apart: 3, of which 2 were waited for; matrix products, arithmetic and copies ran while one was open for 16% of the time, Pallas kernels for 0%

commit v1 on v0

v1 whole, which is shorter than its diff:
```python
import functools

import jax
import jax.numpy as jnp
from jax import lax
from jax.experimental import pallas as pl
from jax.experimental.pallas import tpu as pltpu
from jax.sharding import PartitionSpec as P

QUERY_HEADS = 64
KV_HEADS = 8
HEAD_WIDTH = 128
CHUNK = 8
MESH = pl.DeviceIdType.MESH
F32 = jnp.float32
BF16 = jnp.bfloat16


def offsets_of(n):
    return sorted(range(1, n), key=lambda o: (abs(o - n / 2), o))


def dot(a, b, dims=((1,), (0,))):
    return lax.dot_general(a, b, (dims, ((), ())), preferred_element_type=F32)


def kernel(
    n_a,
    n_t,
    cap,
    q_hbm,
    k_hbm,
    v_hbm,
    kc_hbm,
    vc_hbm,
    len_ref,
    id_ref,
    slot_ref,
    w_hbm,
    down_hbm,
    up_hbm,
    out_ref,
    q_v,
    k_v,
    v_v,
    kc_v,
    vc_v,
    w_v,
    down_v,
    up_v,
    qs,
    att,
    kcf,
    vcf,
    slot_v,
    rows_a,
    part_send,
    part_recv,
    row_send,
    row_recv,
    low_send,
    low_recv,
    back_send,
    back_recv,
    in_sem,
    k_sem,
    v_sem,
    w_sem,
    ps_sem,
    pr_sem,
    rs_sem,
    rr_sem,
    ls_sem,
    lr_sem,
    bs_sem,
    br_sem,
):
    g, a, t = lax.axis_index("groups"), lax.axis_index("adapter"), lax.axis_index("tensor")
    reqs, width = q_v.shape
    span = k_v.shape[1]
    heads = width // HEAD_WIDTH
    kv = kc_v.shape[1] // HEAD_WIDTH
    per = heads // kv
    residents, rank, _ = down_v.shape
    wide = residents * rank
    out_w = w_v.shape[2]
    packed = n_a * cap
    scaling = HEAD_WIDTH ** (-0.5)
    t_order = offsets_of(n_t)

    def on_t(offset):
        return (g, a, lax.rem(t + offset, n_t))

    def on_a(offset):
        return (g, lax.rem(a + offset, n_a), t)

    small = [
        pltpu.make_async_copy(q_hbm, q_v, in_sem.at[0]),
        pltpu.make_async_copy(kc_hbm, kc_v, in_sem.at[1]),
        pltpu.make_async_copy(vc_hbm, vc_v, in_sem.at[2]),
    ]
    down_copy = pltpu.make_async_copy(down_hbm, down_v, in_sem.at[3])
    up_copy = pltpu.make_async_copy(up_hbm, up_v, in_sem.at[4])

    def cache_copies(i):
        part = pl.ds(pl.multiple_of(i * CHUNK, CHUNK), CHUNK)
        return (
            pltpu.make_async_copy(k_hbm.at[part], k_v.at[part], k_sem.at[i]),
            pltpu.make_async_copy(v_hbm.at[part], v_v.at[part], v_sem.at[i]),
        )

    for copy in small:
        copy.start()
    for i in range(reqs // CHUNK):
        for copy in cache_copies(i):
            copy.start()
    w_copies = []
    for s, offset in enumerate(t_order + [0]):
        owner = lax.rem(t + offset, n_t)
        columns = pl.ds(pl.multiple_of(owner * out_w, 128), out_w)
        w_copies.append(pltpu.make_async_copy(w_hbm.at[:, columns], w_v.at[s], w_sem.at[s]))
    for copy in w_copies[:2]:
        copy.start()
    down_copy.start()
    for copy in w_copies[2:]:
        copy.start()
    up_copy.start()

    barrier = pltpu.get_barrier_semaphore()
    for offset in range(1, n_a):
        pl.semaphore_signal(barrier, inc=1, device_id=on_a(offset), device_id_type=MESH)
    for offset in range(1, n_t):
        pl.semaphore_signal(barrier, inc=1, device_id=on_t(offset), device_id_type=MESH)

    for r in range(reqs):
        slot_v[pl.ds(r, 1), :] = jnp.full((1, 128), slot_ref[id_ref[r]], jnp.int32)
    storage = slot_v[...]
    lane = lax.broadcasted_iota(jnp.int32, (reqs, 128), 1)
    holder = storage // residents
    local = storage - holder * residents
    local_hot = (local == lane).astype(F32).astype(BF16)
    away = holder - a
    away = jnp.where(away < 0, away + n_a, away)
    to_hot = away == lane
    before = lax.broadcasted_iota(jnp.int32, (reqs, reqs), 1) < lax.broadcasted_iota(
        jnp.int32, (reqs, reqs), 0
    )
    ranks = dot(before.astype(F32).astype(BF16), to_hot.astype(F32).astype(BF16))
    place = jnp.sum(jnp.where(to_hot, ranks, 0.0), axis=1, keepdims=True).astype(jnp.int32)
    place = place + away[:, :1] * cap
    packing = (
        (place == lax.broadcasted_iota(jnp.int32, (reqs, packed), 1)).astype(F32).astype(BF16)
    )

    for copy in small:
        copy.wait()
    for h in range(heads):
        qs[pl.ds(h, reqs, stride=heads), :] = q_v[
            :, h * HEAD_WIDTH : (h + 1) * HEAD_WIDTH
        ].astype(F32)
    kcf[...] = kc_v[...].astype(F32)
    vcf[...] = vc_v[...].astype(F32)

    def spread(block):
        return jnp.concatenate(
            [
                jnp.broadcast_to(
                    block[j : j + 1, c * HEAD_WIDTH : (c + 1) * HEAD_WIDTH], (per, HEAD_WIDTH)
                )
                for j in range(CHUNK)
                for c in range(kv)
            ],
            axis=0,
        )

    def attend(i, carry):
        k_copy, v_copy = cache_copies(i)
        rows = pl.ds(pl.multiple_of(i * (CHUNK * heads), CHUNK * heads), CHUNK * heads)
        part = pl.ds(pl.multiple_of(i * CHUNK, CHUNK), CHUNK)
        q_f = qs[rows, :]
        row_kv = lax.broadcasted_iota(jnp.int32, (heads, HEAD_WIDTH), 0) // per
        position = lax.broadcasted_iota(jnp.int32, (heads, span), 1)
        fresh = jnp.sum(q_f * spread(kcf[part, :]), axis=1, keepdims=True) * scaling
        k_copy.wait()
        scores = []
        for j in range(CHUNK):
            mine = q_f[j * heads : (j + 1) * heads]
            diag = jnp.concatenate(
                [jnp.where(row_kv == c, mine, 0.0) for c in range(kv)], axis=1
            ).astype(BF16)
            score = dot(diag, k_v[i * CHUNK + j], ((1,), (1,))) * scaling
            scores.append(jnp.where(position < len_ref[i * CHUNK + j], score, -jnp.inf))
        scores = jnp.concatenate(scores, axis=0)
        largest = jnp.maximum(jnp.max(scores, axis=1, keepdims=True), fresh)
        weights = jnp.exp(scores - largest)
        self_weight = jnp.exp(fresh - largest)
        total = jnp.sum(weights, axis=1, keepdims=True) + self_weight
        chances = (weights / total).astype(BF16)
        self_chance = (self_weight / total).astype(BF16).astype(F32)
        v_copy.wait()
        blended = []
        for j in range(CHUNK):
            both = dot(chances[j * heads : (j + 1) * heads], v_v[i * CHUNK + j])
            for c in range(kv):
                blended.append(
                    both[c * per : (c + 1) * per, c * HEAD_WIDTH : (c + 1) * HEAD_WIDTH]
                )
        blended = jnp.concatenate(blended, axis=0) + self_chance * spread(vcf[part, :])
        att[rows, :] = blended
        return carry

    lax.fori_loop(0, reqs // CHUNK, attend, 0)

    for h in range(heads):
        rows_a[:, h * HEAD_WIDTH : (h + 1) * HEAD_WIDTH] = att[
            pl.ds(h, reqs, stride=heads), :
        ].astype(BF16)

    pl.semaphore_wait(barrier, n_a - 1 + n_t - 1)

    step = 512
    for c in range(0, width, step):
        block = dot(packing, rows_a[:, c : c + step], ((0,), (0,))).astype(BF16)
        block = block.reshape(n_a, cap, step)
        row_send[:, :, c : c + step] = block
    row_send[:, :, width:] = (
        dot(packing, local_hot, ((0,), (0,))).astype(BF16).reshape(n_a, cap, 128)
    )
    row_copies = []
    for offset in range(1, n_a):
        copy = pltpu.make_async_remote_copy(
            src_ref=row_send.at[offset],
            dst_ref=row_recv.at[offset],
            send_sem=rs_sem.at[offset],
            recv_sem=rr_sem.at[offset],
            device_id=on_a(offset),
            device_id_type=MESH,
        )
        copy.start()
        row_copies.append(copy)

    part_copies = []

    def project(s, offset):
        w_copies[s].wait()
        half = out_w // 2
        for c in range(0, out_w, half):
            part_send[s, :, c : c + half] = dot(rows_a[...], w_v[s, :, c : c + half]).astype(BF16)
        copy = pltpu.make_async_remote_copy(
            src_ref=part_send.at[s],
            dst_ref=part_recv.at[s],
            send_sem=ps_sem.at[s],
            recv_sem=pr_sem.at[s],
            device_id=on_t(offset),
            device_id_type=MESH,
        )
        copy.start()
        part_copies.append(copy)

    for s, offset in enumerate(t_order):
        project(s, offset)

    down_copy.wait()
    for copy in row_copies:
        copy.wait()
    got = jnp.concatenate([row_send[0][None], row_recv[1:]], axis=0).reshape(packed, width + 128)
    expand = (
        lax.broadcasted_iota(jnp.int32, (128, wide), 1) // rank
        == lax.broadcasted_iota(jnp.int32, (128, wide), 0)
    )
    chosen = dot(got[:, width:], expand.astype(F32).astype(BF16)) > 0.5
    low = dot(got[:, :width], down_v[...].reshape(wide, width), ((1,), (1,)))
    low = jnp.where(chosen, low, 0.0)
    fold = low[:, :128]
    for c in range(128, wide, 128):
        fold = fold + low[:, c : c + 128]
    fold = fold + pltpu.roll(fold, rank, 1)
    left = lax.broadcasted_iota(jnp.int32, (packed // 2, 128), 1) < rank
    own_low = jnp.where(left, fold[: packed // 2], fold[packed // 2 :])
    low_send[...] = own_low.astype(BF16)
    low_copies = []
    for offset in t_order:
        copy = pltpu.make_async_remote_copy(
            src_ref=low_send,
            dst_ref=low_recv.at[offset],
            send_sem=ls_sem.at[offset],
            recv_sem=lr_sem.at[offset],
            device_id=on_t(offset),
            device_id_type=MESH,
        )
        copy.start()
        low_copies.append(copy)

    w_copies[n_t - 1].wait()
    share = dot(rows_a[...], w_v[n_t - 1])

    up_copy.wait()
    for copy in low_copies:
        copy.wait()
    for offset in t_order:
        own_low = own_low + low_recv[offset].astype(F32)
    turned = pltpu.roll(own_low, rank, 1)
    reduced = jnp.concatenate(
        [jnp.where(left, own_low, turned), jnp.where(left, turned, own_low)], axis=0
    )
    reduced = jnp.concatenate([reduced] * (wide // 128), axis=1)
    reduced = jnp.where(chosen, reduced, 0.0).astype(BF16)
    raised = dot(reduced, up_v[...].reshape(wide, out_w)).astype(BF16)
    back_send[...] = raised.reshape(n_a, cap, out_w)
    back_copies = []
    for offset in range(1, n_a):
        copy = pltpu.make_async_remote_copy(
            src_ref=back_send.at[offset],
            dst_ref=back_recv.at[offset],
            send_sem=bs_sem.at[offset],
            recv_sem=br_sem.at[offset],
            device_id=on_a(n_a - offset),
            device_id_type=MESH,
        )
        copy.start()
        back_copies.append(copy)

    for s, copy in enumerate(part_copies):
        copy.wait()
        share = share + part_recv[s].astype(F32)
    for copy in back_copies:
        copy.wait()
    came = jnp.concatenate([back_send[0][None], back_recv[1:]], axis=0).reshape(packed, out_w)
    out_ref[...] = (share + dot(packing, came)).astype(BF16)


def body(n_a, n_t, *operands):
    q, k, v, kc, vc, _, _, _, w, down, up = operands
    reqs, width = q.shape
    out_w = w.shape[1] // n_t
    cap = max(16, 2 * reqs // n_a)
    packed = n_a * cap
    heads = width // HEAD_WIDTH
    chunks = reqs // CHUNK
    dma = pltpu.SemaphoreType.DMA
    hbm = pl.BlockSpec(memory_space=pl.ANY)
    smem = pl.BlockSpec(memory_space=pltpu.SMEM)
    vmem = pltpu.VMEM
    return pl.pallas_call(
        functools.partial(kernel, n_a, n_t, cap),
        out_shape=jax.ShapeDtypeStruct((reqs, out_w), BF16),
        in_specs=[hbm] * 5 + [smem] * 3 + [hbm] * 3,
        out_specs=pl.BlockSpec(memory_space=pltpu.VMEM),
        scratch_shapes=[
            vmem(q.shape, BF16),
            vmem(k.shape, BF16),
            vmem(v.shape, BF16),
            vmem(kc.shape, BF16),
            vmem(vc.shape, BF16),
            vmem((n_t, width, out_w), BF16),
            vmem(down.shape, BF16),
            vmem(up.shape, BF16),
            vmem((reqs * heads, HEAD_WIDTH), F32),
            vmem((reqs * heads, HEAD_WIDTH), F32),
            vmem(kc.shape, F32),
            vmem(vc.shape, F32),
            vmem((reqs, 128), jnp.int32),
            vmem((reqs, width), BF16),
            vmem((n_t - 1, reqs, out_w), BF16),
            vmem((n_t - 1, reqs, out_w), BF16),
            vmem((n_a, cap, width + 128), BF16),
            vmem((n_a, cap, width + 128), BF16),
            vmem((packed // 2, 128), BF16),
            vmem((n_t, packed // 2, 128), BF16),
            vmem((n_a, cap, out_w), BF16),
            vmem((n_a, cap, out_w), BF16),
            dma((5,)),
            dma((chunks,)),
            dma((chunks,)),
            dma((n_t,)),
            dma((n_t,)),
            dma((n_t,)),
            dma((n_a,)),
            dma((n_a,)),
            dma((n_t,)),
            dma((n_t,)),
            dma((n_a,)),
            dma((n_a,)),
        ],
        compiler_params=pltpu.CompilerParams(
            collective_id=0, has_side_effects=True, vmem_limit_bytes=56 * 1024 * 1024
        ),
    )(*operands)


def solution(mesh):
    in_specs = (
        P(("groups", "adapter"), "tensor"),
        P(("groups", "adapter"), None, "tensor"),
        P(("groups", "adapter"), None, "tensor"),
        P(("groups", "adapter"), "tensor"),
        P(("groups", "adapter"), "tensor"),
        P(("groups", "adapter")),
        P(("groups", "adapter")),
        P("groups"),
        P("tensor", None),
        P("adapter", None, "tensor"),
        P("adapter", None, "tensor"),
    )
    out_specs = P(("groups", "adapter"), "tensor")
    run = functools.partial(body, mesh.shape["adapter"], mesh.shape["tensor"])
    return jax.shard_map(run, mesh=mesh, in_specs=in_specs, out_specs=out_specs, check_vma=False)
```

time: 94.1 us -> 35.4 us (0.38)
  Pallas kernels: 0 us -> 33.7 us
  blocking collectives: 26.4 us -> 0 us
  matrix products: 21.7 us -> 0 us
  waiting for transfers between devices: 21.2 us -> 0 us
  between operations: 15.7 us -> 0.01 us
  other arithmetic: 3.65 us -> 0 us
  local copies, waits for them, and re-layouts: 4.92 us -> 1.57 us
    pallas_call x0 -> x1, Pallas kernels: none -> 33.7 us  [body(): pl.pallas_call(functools.partial(kernel, n_a, n_t, cap), out_shape=jax.Sh...]
    dot_general x6 -> x0, matrix products: 21.7 us -> none  [the longest x1 9.78 us: body(): jnp.dot(attended, output_projection, preferred_element_type=jnp.float32)]
    reduce_scatter x2 -> x0, waiting for transfers between devices: 20.2 us -> none  [the longest x1 20.2 us: body(): lax.psum_scatter(unpacked.astype(jnp.bfloat16), 'adapter', scatter_dimens...]
    psum x1 -> x0, blocking collectives: 20 us -> none  [body(): lax.psum(reduced_portion, 'tensor').astype(jnp.bfloat16)]
    unnamed x1 -> x0, blocking collectives: 6.41 us -> none
    convert_element_type x2 -> x0, other arithmetic: 1.68 us -> none  [the longest x1 1.66 us: body(): return (share + adapted).astype(jnp.bfloat16)]
    unnamed x15 -> x1, local copies, waits for them, and re-layouts: 2.62 us -> 1.57 us
    all_gather x1 -> x0, waiting for transfers between devices: 0.96 us -> none  [body(): lax.all_gather(attended, 'adapter', axis=0, tiled=True)]
  transfers between devices with their start and end apart: 3 -> 0, of which waited for: 2 -> 0; matrix products, arithmetic and copies ran while one was open for 16% -> 0% of each run, Pallas kernels for 0% -> 0%
where the time goes in v1:
time: 35.4 us; the launch traced here: 35.3 us
  Pallas kernels  33.7 us (95%)
  local copies, waits for them, and re-layouts  1.57 us (4%)
    pallas_call x1, Pallas kernels, body(): pl.pallas_call(functools.partial(kernel, n_a, n_t, cap), out_shape=jax.Sh...  33.7 us
    unnamed x1, local copies, waits for them, and re-layouts  1.57 us

profile of v1, /device:TPU:0, one launch (start us, length us, event | category | flops | bytes accessed | tf_op | source)
XLA Modules:
  0.0 35.3 jit_solution(12457922465780489400)
XLA Ops:
  0.0 33.7 %shard_map.109 = bf16[64,1024]{1,0:T(8,128)(2,1)} custom-call(bf16[64,2048]{1,0:T(8,128)(2,1)} %q_hbm.1, bf16[64,128,256]{2,1,0:T(8,128)(2,1)} %k_hbm.1, bf16[64,128,256]{2,1,0:T(8,128)(2,1)} %v_hbm.1, bf16[64,256]{1,0:T(8,128)(2,1)} %kc_hbm.1, bf16[64,256]{1,0:T(8,128)(2,1)} %vc_hbm.1, s32[64]{0:T(128)} %len_ref.1, s32[64]{0:T(128)} %id_ref.1, s32[32]{0:T(128)} %slot_ref.1, ...), custom_call_target="tpu_custom_call" | custom-call | tf_op jit(solution)/shard_map/pallas_call | solution.py:344
  33.7 1.6 %copy.13 = bf16[64,1024]{1,0:T(8,128)(2,1)} copy(bf16[64,1024]{1,0:T(8,128)(2,1)} %shard_map.109) | data formatting | bytes 262144

commit v2 on v1

--- a/solution.py
+++ b/solution.py
@@ -10,7 +10,7 @@
 QUERY_HEADS = 64
 KV_HEADS = 8
 HEAD_WIDTH = 128
-CHUNK = 8
+CHUNK = 32
 MESH = pl.DeviceIdType.MESH
 F32 = jnp.float32
 BF16 = jnp.bfloat16
@@ -94,6 +94,12 @@
     def on_a(offset):
         return (g, lax.rem(a + offset, n_a), t)
 
+    barrier = pltpu.get_barrier_semaphore()
+    for offset in range(1, n_a):
+        pl.semaphore_signal(barrier, inc=1, device_id=on_a(offset), device_id_type=MESH)
+    for offset in range(1, n_t):
+        pl.semaphore_signal(barrier, inc=1, device_id=on_t(offset), device_id_type=MESH)
+
     small = [
         pltpu.make_async_copy(q_hbm, q_v, in_sem.at[0]),
         pltpu.make_async_copy(kc_hbm, kc_v, in_sem.at[1]),
@@ -119,18 +125,9 @@
         owner = lax.rem(t + offset, n_t)
         columns = pl.ds(pl.multiple_of(owner * out_w, 128), out_w)
         w_copies.append(pltpu.make_async_copy(w_hbm.at[:, columns], w_v.at[s], w_sem.at[s]))
-    for copy in w_copies[:2]:
-        copy.start()
-    down_copy.start()
-    for copy in w_copies[2:]:
-        copy.start()
-    up_copy.start()
-
-    barrier = pltpu.get_barrier_semaphore()
-    for offset in range(1, n_a):
-        pl.semaphore_signal(barrier, inc=1, device_id=on_a(offset), device_id_type=MESH)
-    for offset in range(1, n_t):
-        pl.semaphore_signal(barrier, inc=1, device_id=on_t(offset), device_id_type=MESH)
+    early = n_t // 2
+    for copy in w_copies[:early]:
+        copy.start()
 
     for r in range(reqs):
         slot_v[pl.ds(r, 1), :] = jnp.full((1, 128), slot_ref[id_ref[r]], jnp.int32)
@@ -238,6 +235,10 @@
         )
         copy.start()
         row_copies.append(copy)
+    for copy in w_copies[early:]:
+        copy.start()
+    down_copy.start()
+    up_copy.start()
 
     part_copies = []
 
@@ -254,11 +255,16 @@
             device_id=on_t(offset),
             device_id_type=MESH,
         )
-        copy.start()
         part_copies.append(copy)
 
+    last = len(t_order) - 1
     for s, offset in enumerate(t_order):
         project(s, offset)
+        if s < last - 1:
+            part_copies[s].start()
+
+    w_copies[n_t - 1].wait()
+    share = dot(rows_a[...], w_v[n_t - 1])
 
     down_copy.wait()
     for copy in row_copies:
@@ -290,9 +296,8 @@
         )
         copy.start()
         low_copies.append(copy)
-
-    w_copies[n_t - 1].wait()
-    share = dot(rows_a[...], w_v[n_t - 1])
+    part_copies[last - 1].start()
+    part_copies[last].start()
 
     up_copy.wait()
     for copy in low_copies:

time: 35.4 us -> 32.2 us (0.910)
  Pallas kernels: 33.7 us -> 30.5 us
    pallas_call x1, Pallas kernels: 33.7 us -> 30.5 us  [body(): pl.pallas_call(functools.partial(kernel, n_a, n_t, cap), out_shape=jax.Sh...]
where the time goes in v2:
time: 32.2 us; the launch traced here: 32.1 us
  Pallas kernels  30.5 us (95%)
  local copies, waits for them, and re-layouts  1.57 us (5%)
    pallas_call x1, Pallas kernels, body(): pl.pallas_call(functools.partial(kernel, n_a, n_t, cap), out_shape=jax.Sh...  30.5 us
    unnamed x1, local copies, waits for them, and re-layouts  1.57 us

profile of v2, /device:TPU:0, one launch (start us, length us, event | category | flops | bytes accessed | tf_op | source)
XLA Modules:
  0.0 32.1 jit_solution(7334413822393740894)
XLA Ops:
  0.0 30.5 %shard_map.109 = bf16[64,1024]{1,0:T(8,128)(2,1)} custom-call(bf16[64,2048]{1,0:T(8,128)(2,1)} %q_hbm.1, bf16[64,128,256]{2,1,0:T(8,128)(2,1)} %k_hbm.1, bf16[64,128,256]{2,1,0:T(8,128)(2,1)} %v_hbm.1, bf16[64,256]{1,0:T(8,128)(2,1)} %kc_hbm.1, bf16[64,256]{1,0:T(8,128)(2,1)} %vc_hbm.1, s32[64]{0:T(128)} %len_ref.1, s32[64]{0:T(128)} %id_ref.1, s32[32]{0:T(128)} %slot_ref.1, ...), custom_call_target="tpu_custom_call" | custom-call | tf_op jit(solution)/shard_map/pallas_call | solution.py:349
  30.5 1.6 %copy.13 = bf16[64,1024]{1,0:T(8,128)(2,1)} copy(bf16[64,1024]{1,0:T(8,128)(2,1)} %shard_map.109) | data formatting | bytes 262144

commit v3 on v2

--- a/solution.py
+++ b/solution.py
@@ -125,7 +125,7 @@
         owner = lax.rem(t + offset, n_t)
         columns = pl.ds(pl.multiple_of(owner * out_w, 128), out_w)
         w_copies.append(pltpu.make_async_copy(w_hbm.at[:, columns], w_v.at[s], w_sem.at[s]))
-    early = n_t // 2
+    early = 1
     for copy in w_copies[:early]:
         copy.start()
 

time: 32.2 us -> 31 us (0.963)
  Pallas kernels: 30.5 us -> 29.3 us
    pallas_call x1, Pallas kernels: 30.5 us -> 29.3 us  [body(): pl.pallas_call(functools.partial(kernel, n_a, n_t, cap), out_shape=jax.Sh...]
where the time goes in v3:
time: 31 us; the launch traced here: 30.9 us
  Pallas kernels  29.3 us (95%)
  local copies, waits for them, and re-layouts  1.57 us (5%)
    pallas_call x1, Pallas kernels, body(): pl.pallas_call(functools.partial(kernel, n_a, n_t, cap), out_shape=jax.Sh...  29.3 us
    unnamed x1, local copies, waits for them, and re-layouts  1.57 us

profile of v3, /device:TPU:0, one launch (start us, length us, event | category | flops | bytes accessed | tf_op | source)
XLA Modules:
  0.0 30.9 jit_solution(6045530401452973467)
XLA Ops:
  0.0 29.3 %shard_map.109 = bf16[64,1024]{1,0:T(8,128)(2,1)} custom-call(bf16[64,2048]{1,0:T(8,128)(2,1)} %q_hbm.1, bf16[64,128,256]{2,1,0:T(8,128)(2,1)} %k_hbm.1, bf16[64,128,256]{2,1,0:T(8,128)(2,1)} %v_hbm.1, bf16[64,256]{1,0:T(8,128)(2,1)} %kc_hbm.1, bf16[64,256]{1,0:T(8,128)(2,1)} %vc_hbm.1, s32[64]{0:T(128)} %len_ref.1, s32[64]{0:T(128)} %id_ref.1, s32[32]{0:T(128)} %slot_ref.1, ...), custom_call_target="tpu_custom_call" | custom-call | tf_op jit(solution)/shard_map/pallas_call | solution.py:349
  29.3 1.6 %copy.13 = bf16[64,1024]{1,0:T(8,128)(2,1)} copy(bf16[64,1024]{1,0:T(8,128)(2,1)} %shard_map.109) | data formatting | bytes 262144
